TPU v7x, 32 devices: a whole 2x2x4 slice. The times are simulated.
32 devices in a mesh: blk: 8 (over z, x), rep: 4 (over y, core).
Axes of the slice: x: 2, y: 2, z: 4, core: 2. Of those that a mesh axis runs over, the one named last changes fastest.
Arguments:
- signals: bfloat16 [8192, 2048], P('rep', 'blk'), may hold values from -6 to 6
- omega: float32 [8, 5, 256, 256], P('blk', None, 'rep'), may hold values from -1.2 to 3, as said below
- pattern: int32 [8, 5], P('blk'), may hold values from 0 to 7, as said below
Outputs:
- omega_next: float32 [8, 5, 256, 256], P('blk', None, 'rep')
Inputs may be any that keep to these rules, and one draw needn't show every extreme that they name: pattern[i, 0] = i. For two distinct whole numbers A and B from 1 to 3, the same in every row, pattern[i, 1] to pattern[i, 4] are i + A, i - A, i + B and i - B modulo 8 in some order, the same order in every row. Omega is symmetric: omega[i, k] is the transpose of omega[pattern[i, k], k2] where pattern[pattern[i, k], k2] = i. The diagonal entries of omega[i, 0] lie between 1 and 3.
All inputs are finite; a program needn't handle non-finite values.
Results may differ from a plain program's by a relative error of at most 0.0033.
Values may be sent and summed in bfloat16 or wider, within the bound.
No kernel may reach another device: no remote copies, remote signals or barrier semaphores. Data moves between devices by JAX's collectives and lax.ppermute only.
A program may use at most 128 MiB of HBM per device.

v0:
```python
import jax
import jax.numpy as jnp
from jax import lax
from jax.sharding import PartitionSpec as P

STEP_SIZE = 0.5
PENALTY = 0.1


def shifted_2(block, axis, distance):
    devices = range(lax.axis_size(axis))
    route = [((i - distance) % len(devices), i) for i in devices]
    return lax.ppermute(block, axis, route)


def advance(stacked, shifted, distance, section_index):
    chosen = jnp.mod(distance // (1 << section_index), 2) == 1
    return jnp.where(chosen[:, None, None], shifted, stacked)


def slot_order(drawn_offsets, team_count):
    slot_ids = jnp.arange(drawn_offsets.shape[0], dtype=jnp.int32)
    partner = jnp.argmax(drawn_offsets == team_count - drawn_offsets[1])
    third = jnp.where(partner == 2, 3, 2).astype(jnp.int32)
    fourth = jnp.where(partner == 4, 3, 4).astype(jnp.int32)
    order = jnp.stack([jnp.zeros((), jnp.int32), jnp.ones((), jnp.int32), partner, third, fourth])
    inverse = jnp.argmax(order[None, :] == slot_ids[:, None], axis=1)
    return (order, inverse)


def per_device(signals, omega, pattern):
    team_count = lax.axis_size("blk")
    replica_count = lax.axis_size("rep")
    level_count = team_count.bit_length() - 1
    team_index = lax.axis_index("blk")
    replica_index = lax.axis_index("rep")
    slot_count = omega.shape[1]
    tile_rows = omega.shape[2]
    tile_width = omega.shape[3]
    time_length = signals.shape[0] * replica_count
    drawn_offsets = jnp.mod(pattern[0] - team_index, team_count)
    order, inverse = slot_order(drawn_offsets, team_count)
    offsets = drawn_offsets[order]
    own_tiles = omega[0][order]
    panels = lax.all_gather(omega.astype(jnp.bfloat16), "rep", axis=2, tiled=True)[0][order]
    remote = jnp.broadcast_to(signals[None], (slot_count - 1,) + signals.shape)
    distance = offsets[1:]
    for section_index in range(level_count):
        shifted = shifted_2(remote, "blk", -(1 << section_index))
        remote = advance(remote, shifted, distance, section_index)
    gathered = jnp.concatenate([signals[None], remote], axis=0)
    mixed = jnp.einsum("ktc,kdc->td", gathered, panels, preferred_element_type=jnp.float32).astype(
        jnp.bfloat16
    )
    left_terms = jnp.einsum("td,ktc->kdc", mixed, gathered, preferred_element_type=jnp.float32)
    stacked = jnp.concatenate([left_terms, jnp.swapaxes(left_terms, 1, 2)], axis=0)
    first_row = replica_index * tile_rows
    summed = lax.psum(stacked, "rep")
    summed = lax.dynamic_slice_in_dim(summed, first_row, tile_rows, 1)
    own_terms = summed[:slot_count]
    flipped = summed[slot_count:]
    mirrored = [
        flipped[slot_index + 1] if slot_index % 2 == 1 else flipped[slot_index - 1]
        for slot_index in range(1, slot_count)
    ]
    outgoing = jnp.stack(mirrored)
    distance = offsets[1:]
    for section_index in range(level_count):
        shifted = shifted_2(outgoing, "blk", -(1 << section_index))
        outgoing = advance(outgoing, shifted, distance, section_index)
    returned = jnp.concatenate([flipped[0:1], outgoing], axis=0)
    gradient = (own_terms + returned) / (2.0 * time_length)
    column_ids = jnp.arange(tile_width, dtype=jnp.int32)
    row_ids = first_row + jnp.arange(tile_rows, dtype=jnp.int32)
    diagonal_mask = column_ids[None, :] == row_ids[:, None]
    diag_values = jnp.sum(jnp.where(diagonal_mask, own_tiles[0], 0.0), axis=1)
    first_grad = gradient[0] - jnp.where(diagonal_mask, (1.0 / diag_values)[:, None], 0.0)
    gradient = jnp.concatenate([first_grad[None], gradient[1:]], axis=0)
    updated = own_tiles - STEP_SIZE * gradient
    shrunk = jnp.sign(updated) * jnp.maximum(jnp.abs(updated) - STEP_SIZE * PENALTY, 0.0)
    slot_ids = jnp.arange(slot_count, dtype=jnp.int32)
    keep_mask = (slot_ids[:, None, None] == 0) & diagonal_mask[None]
    result = jnp.where(keep_mask, updated, shrunk)
    return result[inverse][None]


def solution(mesh):
    return jax.shard_map(
        per_device,
        mesh=mesh,
        in_specs=(P("rep", "blk"), P("blk", None, "rep", None), P("blk", None)),
        out_specs=P("blk", None, "rep", None),
        check_vma=False,
    )
```

profile of v0, /device:TPU:0, one launch (start us, length us, event | category | flops | bytes accessed | tf_op | source)
XLA Modules:
  0.0 501.2 jit_solution(16050896373568523290)
XLA Ops:
  6.5 0.0 copy-start
  6.5 0.0 copy-start.2
  6.5 0.0 all-reduce.2.cloned.1.call-start
  6.5 3.6 broadcast_in_dim.88
  10.1 6.0 %collective-permute-start = (bf16[4,2048,256]{2,1,0:T(8,128)(2,1)}, bf16[4,2048,256]{2,1,0:T(8,128)(2,1)}, u32[]{:S(2)}, u32[]{:S(2)}) collective-permute-start(bf16[4,2048,256]{2,1,0:T(8,128)(2,1)} %broadcast_in_dim.88), channel_id=1, source_target_pairs={{4,0},{8,4},{12,8},{16,12},{20,16},{24,20},{28,24},{0,28},{5,1},{9... | collective-permute-start | bytes 12582920 | tf_op jit(solution)/shard_map/ppermute | solution.py:13
  16.1 0.0 copy-done.2
  16.1 0.6 slice.40
  17.3 0.7 compare_reduce_fusion
  19.1 0.7 stack.26
  19.8 0.6 gather_fusion.1
  20.5 0.1 fusion.10
  20.6 85.6 %collective-permute-done = bf16[4,2048,256]{2,1,0:T(8,128)(2,1)} collective-permute-done((bf16[4,2048,256]{2,1,0:T(8,128)(2,1)}, bf16[4,2048,256]{2,1,0:T(8,128)(2,1)}, u32[]{:S(2)}, u32[]{:S(2)}) %collective-permute-start) | collective-permute-done | bytes 4194336 | tf_op jit(solution)/shard_map/ppermute | solution.py:13
  106.2 0.0 copy-done
  106.2 2.7 broadcast_select_fusion
  108.9 1.6 collective-permute-start.1
  110.5 89.9 %collective-permute-done.1 = bf16[4,2048,256]{2,1,0:T(8,128)(2,1)S(1)} collective-permute-done((bf16[4,2048,256]{2,1,0:T(8,128)(2,1)S(1)}, bf16[4,2048,256]{2,1,0:T(8,128)(2,1)S(1)}, u32[]{:S(2)}, u32[]{:S(2)}) %collective-permute-start.1) | collective-permute-done | bytes 4194336 | tf_op jit(solution)/shard_map/ppermute | solution.py:13
  200.4 4.9 broadcast_select_fusion.1
  205.3 0.5 collective-permute-start.2
  205.9 0.0 copy-done.1
  205.9 7.9 %all_gather.3 = bf16[1,5,256,256]{3,2,1,0:T(8,128)(2,1)S(1)} all-gather(bf16[1,5,64,256]{3,2,1,0:T(8,128)(2,1)S(1)} %convert_element_type.6), channel_id=1, replica_groups=mesh['blk'=8,'rep'=4] {'rep'}, dimensions={2}, use_global_device_ids=true | all-gather | bytes 819200 | tf_op jit(solution)/shard_map/all_gather | solution.py:45
  213.8 0.6 gather_fusion.2
  214.4 172.5 %collective-permute-done.2 = bf16[4,2048,256]{2,1,0:T(8,128)(2,1)} collective-permute-done((bf16[4,2048,256]{2,1,0:T(8,128)(2,1)}, bf16[4,2048,256]{2,1,0:T(8,128)(2,1)}, u32[]{:S(2)}, u32[]{:S(2)}) %collective-permute-start.2) | collective-permute-done | bytes 4194336 | tf_op jit(solution)/shard_map/ppermute | solution.py:13
  387.0 4.0 broadcast_select_fusion.2
  390.9 1.6 fusion.4
  392.6 1.7 fusion
  394.2 1.5 copy.11
  395.7 3.1 pad_maximum_fusion.5
  398.8 0.0 all-reduce.2.cloned.1.call-update
  398.8 0.6 gather_fusion
  399.4 0.7 stack.31
  400.1 0.6 iota_reduce_fusion
  400.7 60.1 %all-reduce.2.cloned.1.call-done = f32[10,256,256]{2,1,0:T(8,128)} async-done(((f32[10,256,256]{2,1,0:T(8,128)}), f32[10,256,256]{2,1,0:T(8,128)}) %all-reduce.2.cloned.1.call-update) | async-done | bytes 2621456 | tf_op jit(solution)/shard_map/psum | solution.py:58
  460.8 1.0 constant_dynamic-slice_fusion.3
  461.8 4.3 collective-permute-start.3
  466.1 0.2 fusion.8
  466.3 5.3 %collective-permute-done.3 = f32[4,64,256]{2,1,0:T(8,128)S(1)} collective-permute-done((f32[4,64,256]{2,1,0:T(8,128)S(1)}, f32[4,64,256]{2,1,0:T(8,128)S(1)}, u32[]{:S(2)}, u32[]{:S(2)}) %collective-permute-start.3) | collective-permute-done | bytes 262176 | tf_op jit(solution)/shard_map/ppermute | solution.py:13
  471.6 0.1 broadcast_select_fusion.3
  471.7 1.6 collective-permute-start.4
  473.3 5.5 %collective-permute-done.4 = f32[4,64,256]{2,1,0:T(8,128)S(1)} collective-permute-done((f32[4,64,256]{2,1,0:T(8,128)S(1)}, f32[4,64,256]{2,1,0:T(8,128)S(1)}, u32[]{:S(2)}, u32[]{:S(2)}) %collective-permute-start.4) | collective-permute-done | bytes 262176 | tf_op jit(solution)/shard_map/ppermute | solution.py:13
  478.8 0.1 broadcast_select_fusion.4
  478.9 0.7 collective-permute-start.5
  479.6 0.1 iota_compare_fusion.1
  479.7 11.9 %collective-permute-done.5 = f32[4,64,256]{2,1,0:T(8,128)S(1)} collective-permute-done((f32[4,64,256]{2,1,0:T(8,128)S(1)}, f32[4,64,256]{2,1,0:T(8,128)S(1)}, u32[]{:S(2)}, u32[]{:S(2)}) %collective-permute-start.5) | collective-permute-done | bytes 262176 | tf_op jit(solution)/shard_map/ppermute | solution.py:13
  491.6 0.1 broadcast_select_fusion.5
  491.7 1.0 fusion.5
  492.8 0.1 slice_subtract_fusion
  492.9 0.2 multiply_select_fusion
  493.1 1.3 gather_fusion.3
  (13 shorter events, 0.1 us)
Async XLA Ops:
  6.5 99.7 %copy-start = (bf16[2048,256]{1,0:T(8,128)(2,1)S(1)}, bf16[2048,256]{1,0:T(8,128)(2,1)}, u32[]{:S(2)}) copy-start(bf16[2048,256]{1,0:T(8,128)(2,1)} %param.3) | copy-start | bytes 3145732
  6.5 9.5 %copy-start.2 = (s32[1,5]{1,0:T(1,128)S(1)}, s32[1,5]{1,0:T(1,128)}, u32[]{:S(2)}) copy-start(s32[1,5]{1,0:T(1,128)} %param.5) | copy-start | bytes 64
  6.5 454.2 %all-reduce.2.cloned.1.call-start = ((), (), s32[]{:S(2)}) async-start(), calls=%async_computation | async-start | bytes 5242880 | tf_op jit(solution)/shard_map/psum | solution.py:58
  10.1 96.1 %collective-permute-start = (bf16[4,2048,256]{2,1,0:T(8,128)(2,1)}, bf16[4,2048,256]{2,1,0:T(8,128)(2,1)}, u32[]{:S(2)}, u32[]{:S(2)}) collective-permute-start(bf16[4,2048,256]{2,1,0:T(8,128)(2,1)} %broadcast_in_dim.88), channel_id=1, source_target_pairs={{4,0},{8,4},{12,8},{16,12},{20,16},{24,20},{28,24},{0,28},{5,1},{9... | collective-permute-start | bytes 12582920 | tf_op jit(solution)/shard_map/ppermute | solution.py:13
  108.9 91.5 %collective-permute-start.1 = (bf16[4,2048,256]{2,1,0:T(8,128)(2,1)S(1)}, bf16[4,2048,256]{2,1,0:T(8,128)(2,1)S(1)}, u32[]{:S(2)}, u32[]{:S(2)}) collective-permute-start(bf16[4,2048,256]{2,1,0:T(8,128)(2,1)S(1)} %broadcast_select_fusion), channel_id=1, source_target_pairs={{8,0},{12,4},{16,8},{20,12},{24,16},{28,20},{0,24},{4,28},{9,1},{1... | collective-permute-start | bytes 12582920 | tf_op jit(solution)/shard_map/ppermute | solution.py:13
  200.4 5.5 %copy-start.1 = (f32[1,5,64,256]{3,2,1,0:T(8,128)S(1)}, f32[1,5,64,256]{3,2,1,0:T(8,128)}, u32[]{:S(2)}) copy-start(f32[1,5,64,256]{3,2,1,0:T(8,128)} %param.4) | copy-start | bytes 983044
  205.3 181.6 %collective-permute-start.2 = (bf16[4,2048,256]{2,1,0:T(8,128)(2,1)}, bf16[4,2048,256]{2,1,0:T(8,128)(2,1)}, u32[]{:S(2)}, u32[]{:S(2)}) collective-permute-start(bf16[4,2048,256]{2,1,0:T(8,128)(2,1)} %broadcast_select_fusion.1), channel_id=1, source_target_pairs={{16,0},{20,4},{24,8},{28,12},{0,16},{4,20},{8,24},{12,28},{17,1},{... | collective-permute-start | bytes 12582920 | tf_op jit(solution)/shard_map/ppermute | solution.py:13
  461.8 9.8 %collective-permute-start.3 = (f32[4,64,256]{2,1,0:T(8,128)S(1)}, f32[4,64,256]{2,1,0:T(8,128)S(1)}, u32[]{:S(2)}, u32[]{:S(2)}) collective-permute-start(f32[4,64,256]{2,1,0:T(8,128)S(1)} %pad_maximum_fusion.10), channel_id=1, source_target_pairs={{4,0},{8,4},{12,8},{16,12},{20,16},{24,20},{28,24},{0,28},{5,1},{9... | collective-permute-start | bytes 786440 | tf_op jit(solution)/shard_map/ppermute | solution.py:13
  471.7 7.1 %collective-permute-start.4 = (f32[4,64,256]{2,1,0:T(8,128)S(1)}, f32[4,64,256]{2,1,0:T(8,128)S(1)}, u32[]{:S(2)}, u32[]{:S(2)}) collective-permute-start(f32[4,64,256]{2,1,0:T(8,128)S(1)} %broadcast_select_fusion.3), channel_id=1, source_target_pairs={{8,0},{12,4},{16,8},{20,12},{24,16},{28,20},{0,24},{4,28},{9,1},{1... | collective-permute-start | bytes 786440 | tf_op jit(solution)/shard_map/ppermute | solution.py:13
  478.9 12.7 %collective-permute-start.5 = (f32[4,64,256]{2,1,0:T(8,128)S(1)}, f32[4,64,256]{2,1,0:T(8,128)S(1)}, u32[]{:S(2)}, u32[]{:S(2)}) collective-permute-start(f32[4,64,256]{2,1,0:T(8,128)S(1)} %broadcast_select_fusion.4), channel_id=1, source_target_pairs={{16,0},{20,4},{24,8},{28,12},{0,16},{4,20},{8,24},{12,28},{17,1},{... | collective-permute-start | bytes 786440 | tf_op jit(solution)/shard_map/ppermute | solution.py:13
Sparse Core Ops, SparseCore 0:
  398.9 61.7 all-reduce.1
where the time goes:
time: 502 us; the launch traced here: 501 us
  waiting for transfers between devices  431 us (86%)
  other arithmetic  17.9 us (4%)
  between operations  15.3 us (3%)
  starting transfers between devices  14.8 us (3%)
  local copies, waits for them, and re-layouts  11.1 us (2%)
  blocking collectives  7.91 us (2%)
    ppermute x6, waiting for transfers between devices, shifted_2(): return lax.ppermute(block, axis, route)  371 us
    psum x1, waiting for transfers between devices, per_device(): summed = lax.psum(stacked, 'rep')  60.1 us
    ppermute x6, starting transfers between devices, shifted_2(): return lax.ppermute(block, axis, route)  14.8 us
    select_n x6, other arithmetic, advance(): return jnp.where(chosen[:, None, None], shifted, stacked)  11.9 us
  transfers between devices with their start and end apart: 7, of which 7 were waited for; matrix products, arithmetic and copies ran while one was open for 1% of the time, Pallas kernels for 0%

commit v1 on v0

v1 whole, which is shorter than its diff:
```python
import functools

import jax
import jax.numpy as jnp
from jax import lax
from jax.experimental import pallas as pl
from jax.experimental.pallas import tpu as pltpu
from jax.sharding import PartitionSpec as P

STEP_SIZE = 0.5
PENALTY = 0.1
LOW = 2
VMEM_LIMIT = 56 * 2**20
F32 = jnp.float32
BF16 = jnp.bfloat16

VMEM = pl.BlockSpec(memory_space=pltpu.VMEM)
SMEM = pl.BlockSpec(memory_space=pltpu.SMEM)
PARAMS = pltpu.CompilerParams(vmem_limit_bytes=VMEM_LIMIT)


def stored_offsets(pattern_ref, team, teams):
    drawn = [lax.rem(pattern_ref[0, k] - team + teams, teams) for k in range(1, 5)]
    a = functools.reduce(jnp.minimum, drawn)
    b = functools.reduce(jnp.minimum, [jnp.where(d == a, teams, d) for d in drawn])
    offsets = [jnp.int32(0), a, b, teams - b, teams - a]
    slots = [jnp.int32(0)]
    for offset in offsets[1:]:
        slots.append(sum(jnp.where(d == offset, k + 1, 0) for k, d in enumerate(drawn)))
    return offsets, slots


def weights_kernel(teams, place_ref, pattern_ref, omega_ref, out_ref):
    _, slots = stored_offsets(pattern_ref, place_ref[0], teams)
    for k in range(3):
        out_ref[k] = omega_ref[0, slots[k]].astype(BF16)


def product_kernel(teams, replicas, tile_rows, place_ref, pattern_ref, own_ref, other_ref, omega_ref, *rest):
    chips = replicas // 2
    outs = rest[: LOW * chips]
    mixed_ref, flip_ref, left_ref = rest[LOW * chips :]
    team, replica = place_ref[0], place_ref[1]
    core, chip = lax.rem(replica, 2), lax.div(replica, 2)
    offsets, _ = stored_offsets(pattern_ref, team, teams)
    times, width = own_ref.shape[1], own_ref.shape[2]

    def block(c):
        return jnp.concatenate([own_ref[c], other_ref[c]], axis=0)

    def tile(i, k):
        return omega_ref[i, :, k].reshape(width, width)

    nn = (((1,), (0,)), ((), ()))
    nt = (((1,), (1,)), ((), ()))

    def mix(i, carry):
        total = None
        for k, offset in enumerate(offsets):
            c = lax.rem(i + offset, teams)
            if k < 3:
                term = lax.dot_general(block(c), tile(i, k), nt, preferred_element_type=F32)
            else:
                term = lax.dot_general(block(c), tile(c, 5 - k), nn, preferred_element_type=F32)
            total = term if total is None else total + term
        mixed = total.astype(BF16)
        mixed_ref[i] = mixed
        flip_ref[:, : 2 * times] = mixed.T
        flip_ref[:, 2 * times :] = block(i).T
        for m in range(chips):
            row = (2 * (chip ^ m) + core) * tile_rows
            left_ref[i, m * tile_rows : (m + 1) * tile_rows] = flip_ref[
                pl.ds(pl.multiple_of(row, tile_rows), tile_rows)
            ]
        return carry

    unroll = teams <= 8
    lax.fori_loop(0, teams, mix, 0, unroll=unroll)
    for mx in range(LOW):

        def outer(z, carry):
            i = z * LOW + (lax.rem(team, LOW) ^ mx)
            for k, offset in enumerate(offsets):
                c = lax.rem(i + offset, teams)
                right = jnp.concatenate([own_ref[c], other_ref[c], mixed_ref[c]], axis=0)
                part = lax.dot_general(left_ref[i], right, nn, preferred_element_type=F32).astype(BF16)
                for m in range(chips):
                    outs[mx * chips + m][z, k] = part[m * tile_rows : (m + 1) * tile_rows]
            return carry

        lax.fori_loop(0, teams // LOW, outer, 0, unroll=unroll)


def add_kernel(teams, place_ref, *rest):
    count = teams // LOW
    parts, outs = rest[:-count], rest[-count:]
    z = lax.div(place_ref[0], LOW)
    for m in range(count):
        total = parts[0][z ^ m].astype(F32)
        for part in parts[1:]:
            total = total + part[z ^ m].astype(F32)
        outs[m][...] = total.astype(outs[m].dtype)


def update_kernel(teams, scale, place_ref, pattern_ref, omega_ref, *rest):
    parts, out_ref = rest[:-1], rest[-1]
    _, slots = stored_offsets(pattern_ref, place_ref[0], teams)
    rows, width = out_ref.shape[2:]
    first = place_ref[1] * rows
    row_ids = first + lax.broadcasted_iota(jnp.int32, (rows, width), 0)
    diagonal = row_ids == lax.broadcasted_iota(jnp.int32, (rows, width), 1)
    for k in range(5):
        total = parts[0][k].astype(F32)
        for part in parts[1:]:
            total = total + part[k].astype(F32)
        current = omega_ref[0, slots[k]]
        gradient = total * scale
        if k == 0:
            gradient = gradient - jnp.where(diagonal, 1.0 / current, 0.0)
        value = current - STEP_SIZE * gradient
        bound = STEP_SIZE * PENALTY
        shrunk = jnp.where(value > bound, value - bound, jnp.where(value < -bound, value + bound, 0.0))
        if k == 0:
            shrunk = jnp.where(diagonal, value, shrunk)
        out_ref[0, slots[k]] = shrunk


def per_device(teams, replicas, signals, omega, pattern):
    chips = replicas // 2
    slots, tile_rows, width = omega.shape[1:]
    times = signals.shape[0] // teams
    place = jnp.stack([lax.axis_index("blk"), lax.axis_index("rep")]).astype(jnp.int32)

    def swap(array, blk_mask, rep_mask):
        route = [
            (b * replicas + r, (b ^ blk_mask) * replicas + (r ^ rep_mask))
            for b in range(teams)
            for r in range(replicas)
        ]
        return lax.ppermute(array, ("blk", "rep"), route)

    upper = pl.pallas_call(
        functools.partial(weights_kernel, teams),
        out_shape=jax.ShapeDtypeStruct((3, tile_rows, width), BF16),
        in_specs=[SMEM, SMEM, VMEM],
        out_specs=VMEM,
        compiler_params=PARAMS,
        name="weights",
    )(place, pattern, omega)
    weights = lax.all_gather(upper, ("blk", "rep")).reshape(teams, replicas, 3, tile_rows, width)

    own = lax.all_to_all(signals.reshape(teams, times, width), "blk", 0, 0)
    other = swap(own, 0, 1)

    planes = LOW * chips
    count = teams // LOW
    partial = pl.pallas_call(
        functools.partial(product_kernel, teams, replicas, tile_rows),
        out_shape=[jax.ShapeDtypeStruct((count, slots, tile_rows, width), BF16)] * planes,
        in_specs=[SMEM, SMEM, VMEM, VMEM, VMEM],
        out_specs=[VMEM] * planes,
        scratch_shapes=[
            pltpu.VMEM((teams, 2 * times, width), BF16),
            pltpu.VMEM((width, 4 * times), BF16),
            pltpu.VMEM((teams, chips * tile_rows, 4 * times), BF16),
        ],
        compiler_params=PARAMS,
        name="products",
    )(place, pattern, own, other, weights)
    received = [
        swap(partial[mx * chips + my], mx, 2 * my) if mx + my else partial[0]
        for mx in range(LOW)
        for my in range(chips)
    ]

    summed = pl.pallas_call(
        functools.partial(add_kernel, teams),
        out_shape=[
            jax.ShapeDtypeStruct((slots, tile_rows, width), BF16 if m else F32) for m in range(count)
        ],
        in_specs=[SMEM] + [VMEM] * planes,
        out_specs=[VMEM] * count,
        compiler_params=PARAMS,
        name="plane_sum",
    )(place, *received)
    arrived = [swap(summed[m], m * LOW, 0) if m else summed[0] for m in range(count)]

    scale = 1.0 / (2.0 * signals.shape[0] * replicas)
    return pl.pallas_call(
        functools.partial(update_kernel, teams, scale),
        out_shape=jax.ShapeDtypeStruct(omega.shape, F32),
        in_specs=[SMEM, SMEM, VMEM] + [VMEM] * count,
        out_specs=VMEM,
        compiler_params=PARAMS,
        name="update",
    )(place, pattern, omega, *arrived)


def solution(mesh):
    return jax.shard_map(
        functools.partial(per_device, mesh.shape["blk"], mesh.shape["rep"]),
        mesh=mesh,
        in_specs=(P("rep", "blk"), P("blk", None, "rep", None), P("blk", None)),
        out_specs=P("blk", None, "rep", None),
        check_vma=False,
    )
```

time: 502 us -> 145 us (0.29)
  waiting for transfers between devices: 431 us -> 68.6 us
  blocking collectives: 7.91 us -> 36.5 us
  other arithmetic: 17.9 us -> 0.59 us
  Pallas kernels: 0 us -> 16.6 us
  local copies, waits for them, and re-layouts: 11.1 us -> 1.56 us
  starting transfers between devices: 14.8 us -> 7.88 us
    ppermute x6 -> x7, waiting for transfers between devices: 371 us -> 42.4 us  [swap(): return lax.ppermute(array, ('blk', 'rep'), route)]
    psum x1 -> x0, waiting for transfers between devices: 60.1 us -> none  [per_device(): summed = lax.psum(stacked, 'rep')]
    all_to_all x0 -> x1, blocking collectives: none -> 36.5 us  [per_device(): own = lax.all_to_all(signals.reshape(teams, times, width), 'blk', 0, 0)]
    all_gather x0 -> x1, waiting for transfers between devices: none -> 26.1 us  [per_device(): lax.all_gather(upper, ('blk', 'rep'))]
    pallas_call x0 -> x4, Pallas kernels: none -> 16.6 us  [the longest x1 10 us: per_device(): pl.pallas_call(functools.partial(product_kernel, teams, replicas, tile_ro...]
    select_n x10 -> x0, other arithmetic: 12.1 us -> none  [the longest x6 11.9 us: advance(): return jnp.where(chosen[:, None, None], shifted, stacked)]
    all_gather x1 -> x0, blocking collectives: 7.91 us -> none  [per_device(): lax.all_gather(omega.astype(jnp.bfloat16), 'rep', axis=2, tiled=True)[0]]
    ppermute x6 -> x7, starting transfers between devices: 14.8 us -> 7.88 us  [swap(): return lax.ppermute(array, ('blk', 'rep'), route)]
  transfers between devices with their start and end apart: 7 -> 8, of which waited for: 7 -> 7; matrix products, arithmetic and copies ran while one was open for 1% -> 0% of each run, Pallas kernels for 0% -> 0%
where the time goes in v1:
time: 145 us
  waiting for transfers between devices  68.6 us (47%)
  blocking collectives  36.5 us (25%)
  Pallas kernels  16.6 us (11%)
  between operations  13.4 us (9%)
  starting transfers between devices  7.88 us (5%)
  local copies, waits for them, and re-layouts  1.56 us (1%)
    ppermute x7, waiting for transfers between devices, swap(): return lax.ppermute(array, ('blk', 'rep'), route)  42.4 us
    all_to_all x1, blocking collectives, per_device(): own = lax.all_to_all(signals.reshape(teams, times, width), 'blk', 0, 0)  36.5 us
    all_gather x1, waiting for transfers between devices, per_device(): lax.all_gather(upper, ('blk', 'rep'))  26.1 us
    pallas_call x1, Pallas kernels, per_device(): pl.pallas_call(functools.partial(product_kernel, teams, replicas, tile_ro...  10 us
    ppermute x7, starting transfers between devices, swap(): return lax.ppermute(array, ('blk', 'rep'), route)  7.88 us
  transfers between devices with their start and end apart: 8, of which 7 were waited for; matrix products, arithmetic and copies ran while one was open for 0% of the time, Pallas kernels for 0%

profile of v1, /device:TPU:0, one launch (start us, length us, event | category | flops | bytes accessed | tf_op | source)
XLA Modules:
  0.0 145.2 jit_solution(204701910624769384)
XLA Ops:
  6.5 0.0 all-gather.3.cloned.1.call-start
  6.5 0.6 pad_add_fusion.place_ref
  7.1 1.7 %weights.1 = bf16[3,64,256]{2,1,0:T(8,128)(2,1)} custom-call(s32[2]{0:T(128)} %pad_add_fusion.place_ref, s32[1,5]{1,0:T(1,128)} %pattern_ref.5, f32[1,5,64,256]{3,2,1,0:T(8,128)} %omega_ref.3), custom_call_target="tpu_custom_call" | custom-call | tf_op jit(solution)/shard_map/weights/pallas_call | solution.py:142
  8.8 0.0 all-gather.3.cloned.1.call-update
  8.8 36.5 %all_to_all.5.own_ref = bf16[8,256,256]{2,1,0:T(8,128)(2,1)S(1)} all-to-all(bf16[8,256,256]{2,1,0:T(8,128)(2,1)} %bitcast.5), channel_id=1, replica_groups=mesh['blk'=8,'rep'=4] {'blk'}, dimensions={0} | all-to-all | bytes 2097152 | tf_op jit(solution)/shard_map/all_to_all | solution.py:152
  45.4 0.0 copy-start
  45.4 0.0 collective-permute-start
  45.4 2.7 %collective-permute-done.other_ref = bf16[8,256,256]{2,1,0:T(8,128)(2,1)S(1)} collective-permute-done((bf16[8,256,256]{2,1,0:T(8,128)(2,1)S(1)}, bf16[8,256,256]{2,1,0:T(8,128)(2,1)S(1)}, u32[]{:S(2)}, u32[]{:S(2)}) %collective-permute-start) | collective-permute-done | bytes 1048608 | tf_op jit(solution)/shard_map/ppermute | solution.py:140
  48.0 0.0 copy-start.1
  48.0 26.1 %all-gather.3.cloned.1.call-done = bf16[96,64,256]{2,1,0:T(8,128)(2,1)} async-done(((bf16[3,64,256]{2,1,0:T(8,128)(2,1)}), bf16[96,64,256]{2,1,0:T(8,128)(2,1)}) %all-gather.3.cloned.1.call-update) | async-done | bytes 3145744 | tf_op jit(solution)/shard_map/all_gather | solution.py:150
  74.2 0.0 copy-done
  74.2 0.0 copy-done.1
  74.2 10.0 %products.1 = (bf16[4,5,64,256]{3,2,1,0:T(8,128)(2,1)}, bf16[4,5,64,256]{3,2,1,0:T(8,128)(2,1)}, bf16[4,5,64,256]{3,2,1,0:T(8,128)(2,1)}, bf16[4,5,64,256]{3,2,1,0:T(8,128)(2,1)}) custom-call(s32[2]{0:T(128)} %pad_add_fusion.place_ref, s32[1,5]{1,0:T(1,128)} %pattern_ref.5, bf16[8,256,256]{2,1,0:T(8,128)(2,1)} %copy-done, bf16[8,256,256]{2,1,0:T(8,128)(2,1)} %copy-done.1, ...), custom_call_target="tpu_custom_call" | custom-call | tf_op jit(solution)/shard_map/products/pallas_call | solution.py:157
  84.2 1.5 %collective-permute-start.1 = (bf16[4,5,64,256]{3,2,1,0:T(8,128)(2,1)}, bf16[4,5,64,256]{3,2,1,0:T(8,128)(2,1)S(1)}, u32[]{:S(2)}, u32[]{:S(2)}) collective-permute-start(bf16[4,5,64,256]{3,2,1,0:T(8,128)(2,1)} %get-tuple-element.14), channel_id=1, source_target_pairs={{0,2},{1,3},{2,0},{3,1},{4,6},{5,7},{6,4},{7,5},{8,10},{9,11},{10,... | collective-permute-start | bytes 1966088 | tf_op jit(solution)/shard_map/ppermute | solution.py:140
  85.7 0.6 collective-permute-start.2
  86.2 1.5 %collective-permute-start.3 = (bf16[4,5,64,256]{3,2,1,0:T(8,128)(2,1)}, bf16[4,5,64,256]{3,2,1,0:T(8,128)(2,1)S(1)}, u32[]{:S(2)}, u32[]{:S(2)}) collective-permute-start(bf16[4,5,64,256]{3,2,1,0:T(8,128)(2,1)} %get-tuple-element.16), channel_id=1, source_target_pairs={{0,6},{1,7},{2,4},{3,5},{4,2},{5,3},{6,0},{7,1},{8,14},{9,15},{10,... | collective-permute-start | bytes 1966088 | tf_op jit(solution)/shard_map/ppermute | solution.py:140
  87.7 13.6 %collective-permute-done.1.rest_1_ = bf16[4,5,64,256]{3,2,1,0:T(8,128)(2,1)S(1)} collective-permute-done((bf16[4,5,64,256]{3,2,1,0:T(8,128)(2,1)}, bf16[4,5,64,256]{3,2,1,0:T(8,128)(2,1)S(1)}, u32[]{:S(2)}, u32[]{:S(2)}) %collective-permute-start.1) | collective-permute-done | bytes 655392 | tf_op jit(solution)/shard_map/ppermute | solution.py:140
  101.3 0.0 copy-start.2
  101.3 2.2 %collective-permute-done.2.rest_2_ = bf16[4,5,64,256]{3,2,1,0:T(8,128)(2,1)S(1)} collective-permute-done((bf16[4,5,64,256]{3,2,1,0:T(8,128)(2,1)}, bf16[4,5,64,256]{3,2,1,0:T(8,128)(2,1)S(1)}, u32[]{:S(2)}, u32[]{:S(2)}) %collective-permute-start.2) | collective-permute-done | bytes 655392 | tf_op jit(solution)/shard_map/ppermute | solution.py:140
  103.5 0.0 copy-start.3
  103.5 13.1 %collective-permute-done.3.rest_3_ = bf16[4,5,64,256]{3,2,1,0:T(8,128)(2,1)S(1)} collective-permute-done((bf16[4,5,64,256]{3,2,1,0:T(8,128)(2,1)}, bf16[4,5,64,256]{3,2,1,0:T(8,128)(2,1)S(1)}, u32[]{:S(2)}, u32[]{:S(2)}) %collective-permute-start.3) | collective-permute-done | bytes 655392 | tf_op jit(solution)/shard_map/ppermute | solution.py:140
  116.5 0.0 copy-start.4
  116.5 0.0 copy-done.2
  116.5 0.0 copy-done.3
  116.5 0.8 copy-done.4
  117.4 2.8 %plane_sum.1 = (f32[5,64,256]{2,1,0:T(8,128)}, bf16[5,64,256]{2,1,0:T(8,128)(2,1)}, bf16[5,64,256]{2,1,0:T(8,128)(2,1)}, bf16[5,64,256]{2,1,0:T(8,128)(2,1)}) custom-call(s32[2]{0:T(128)} %pad_add_fusion.place_ref, bf16[4,5,64,256]{3,2,1,0:T(8,128)(2,1)} %get-tuple-element.13.rest_0_, bf16[4,5,64,256]{3,2,1,0:T(8,128)(2,1)} %copy-done.2, ...), custom_call_target="tpu_custom_call" | custom-call | tf_op jit(solution)/shard_map/plane_sum/pallas_call | solution.py:176
  120.1 0.5 collective-permute-start.4
  120.7 2.2 %collective-permute-start.5 = (bf16[5,64,256]{2,1,0:T(8,128)(2,1)}, bf16[5,64,256]{2,1,0:T(8,128)(2,1)S(1)}, u32[]{:S(2)}, u32[]{:S(2)}) collective-permute-start(bf16[5,64,256]{2,1,0:T(8,128)(2,1)} %get-tuple-element.19), channel_id=1, source_target_pairs={{0,16},{1,17},{2,18},{3,19},{4,20},{5,21},{6,22},{7,23},{8,24},{9,... | collective-permute-start | bytes 491528 | tf_op jit(solution)/shard_map/ppermute | solution.py:140
  122.8 1.7 %collective-permute-start.6 = (bf16[5,64,256]{2,1,0:T(8,128)(2,1)}, bf16[5,64,256]{2,1,0:T(8,128)(2,1)S(1)}, u32[]{:S(2)}, u32[]{:S(2)}) collective-permute-start(bf16[5,64,256]{2,1,0:T(8,128)(2,1)} %get-tuple-element.20), channel_id=1, source_target_pairs={{0,24},{1,25},{2,26},{3,27},{4,28},{5,29},{6,30},{7,31},{8,16},{9,... | collective-permute-start | bytes 491528 | tf_op jit(solution)/shard_map/ppermute | solution.py:140
  124.5 3.4 %collective-permute-done.4.rest_1_ = bf16[5,64,256]{2,1,0:T(8,128)(2,1)S(1)} collective-permute-done((bf16[5,64,256]{2,1,0:T(8,128)(2,1)}, bf16[5,64,256]{2,1,0:T(8,128)(2,1)S(1)}, u32[]{:S(2)}, u32[]{:S(2)}) %collective-permute-start.4) | collective-permute-done | bytes 163872 | tf_op jit(solution)/shard_map/ppermute | solution.py:140
  127.9 0.0 copy-start.5
  127.9 7.5 %collective-permute-done.5.rest_2_ = bf16[5,64,256]{2,1,0:T(8,128)(2,1)S(1)} collective-permute-done((bf16[5,64,256]{2,1,0:T(8,128)(2,1)}, bf16[5,64,256]{2,1,0:T(8,128)(2,1)S(1)}, u32[]{:S(2)}, u32[]{:S(2)}) %collective-permute-start.5) | collective-permute-done | bytes 163872 | tf_op jit(solution)/shard_map/ppermute | solution.py:140
  135.5 0.0 copy-start.6
  135.5 0.0 collective-permute-done.6.rest_3_
  135.5 0.0 copy-start.7
  135.5 0.0 copy-done.5
  135.5 0.7 copy-done.6
  136.1 0.1 copy-done.7
  136.2 2.2 %update.1 = f32[1,5,64,256]{3,2,1,0:T(8,128)} custom-call(s32[2]{0:T(128)} %pad_add_fusion.place_ref, s32[1,5]{1,0:T(1,128)} %pattern_ref.5, f32[1,5,64,256]{3,2,1,0:T(8,128)} %omega_ref.3, f32[5,64,256]{2,1,0:T(8,128)} %get-tuple-element.17.rest_0_, bf16[5,64,256]{2,1,0:T(8,128)(2,1)} %copy-done.5, bf16[5,64,256]{2,1,0:T(8,128)(2,1)} %copy-done.6, ...), custom_call_target="tpu_custom_call" | custom-call | tf_op jit(solution)/shard_map/update/pallas_call | solution.py:189
Async XLA Ops:
  6.5 67.6 %all-gather.3.cloned.1.call-start = ((), (), s32[]{:S(2)}) async-start(), calls=%async_computation.1 | async-start | bytes 3244032 | tf_op jit(solution)/shard_map/all_gather | solution.py:150
  45.4 28.8 %copy-start = (bf16[8,256,256]{2,1,0:T(8,128)(2,1)}, bf16[8,256,256]{2,1,0:T(8,128)(2,1)S(1)}, u32[]{:S(2)}) copy-start(bf16[8,256,256]{2,1,0:T(8,128)(2,1)S(1)} %all_to_all.5.own_ref) | copy-start | bytes 3145732
  45.4 2.7 %collective-permute-start = (bf16[8,256,256]{2,1,0:T(8,128)(2,1)S(1)}, bf16[8,256,256]{2,1,0:T(8,128)(2,1)S(1)}, u32[]{:S(2)}, u32[]{:S(2)}) collective-permute-start(bf16[8,256,256]{2,1,0:T(8,128)(2,1)S(1)} %all_to_all.5.own_ref), channel_id=1, source_target_pairs={{0,1},{1,0},{2,3},{3,2},{4,5},{5,4},{6,7},{7,6},{8,9},{9,8},{10,11... | collective-permute-start | bytes 3145736 | tf_op jit(solution)/shard_map/ppermute | solution.py:140
  48.0 26.2 %copy-start.1 = (bf16[8,256,256]{2,1,0:T(8,128)(2,1)}, bf16[8,256,256]{2,1,0:T(8,128)(2,1)S(1)}, u32[]{:S(2)}) copy-start(bf16[8,256,256]{2,1,0:T(8,128)(2,1)S(1)} %collective-permute-done.other_ref) | copy-start | bytes 3145732
  84.2 17.1 %collective-permute-start.1 = (bf16[4,5,64,256]{3,2,1,0:T(8,128)(2,1)}, bf16[4,5,64,256]{3,2,1,0:T(8,128)(2,1)S(1)}, u32[]{:S(2)}, u32[]{:S(2)}) collective-permute-start(bf16[4,5,64,256]{3,2,1,0:T(8,128)(2,1)} %get-tuple-element.14), channel_id=1, source_target_pairs={{0,2},{1,3},{2,0},{3,1},{4,6},{5,7},{6,4},{7,5},{8,10},{9,11},{10,... | collective-permute-start | bytes 1966088 | tf_op jit(solution)/shard_map/ppermute | solution.py:140
  85.7 17.8 %collective-permute-start.2 = (bf16[4,5,64,256]{3,2,1,0:T(8,128)(2,1)}, bf16[4,5,64,256]{3,2,1,0:T(8,128)(2,1)S(1)}, u32[]{:S(2)}, u32[]{:S(2)}) collective-permute-start(bf16[4,5,64,256]{3,2,1,0:T(8,128)(2,1)} %get-tuple-element.15), channel_id=1, source_target_pairs={{0,4},{1,5},{2,6},{3,7},{4,0},{5,1},{6,2},{7,3},{8,12},{9,13},{10,... | collective-permute-start | bytes 1966088 | tf_op jit(solution)/shard_map/ppermute | solution.py:140
  86.2 30.3 %collective-permute-start.3 = (bf16[4,5,64,256]{3,2,1,0:T(8,128)(2,1)}, bf16[4,5,64,256]{3,2,1,0:T(8,128)(2,1)S(1)}, u32[]{:S(2)}, u32[]{:S(2)}) collective-permute-start(bf16[4,5,64,256]{3,2,1,0:T(8,128)(2,1)} %get-tuple-element.16), channel_id=1, source_target_pairs={{0,6},{1,7},{2,4},{3,5},{4,2},{5,3},{6,0},{7,1},{8,14},{9,15},{10,... | collective-permute-start | bytes 1966088 | tf_op jit(solution)/shard_map/ppermute | solution.py:140
  101.3 15.2 %copy-start.2 = (bf16[4,5,64,256]{3,2,1,0:T(8,128)(2,1)}, bf16[4,5,64,256]{3,2,1,0:T(8,128)(2,1)S(1)}, u32[]{:S(2)}) copy-start(bf16[4,5,64,256]{3,2,1,0:T(8,128)(2,1)S(1)} %collective-permute-done.1.rest_1_) | copy-start | bytes 1966084
  103.5 13.1 %copy-start.3 = (bf16[4,5,64,256]{3,2,1,0:T(8,128)(2,1)}, bf16[4,5,64,256]{3,2,1,0:T(8,128)(2,1)S(1)}, u32[]{:S(2)}) copy-start(bf16[4,5,64,256]{3,2,1,0:T(8,128)(2,1)S(1)} %collective-permute-done.2.rest_2_) | copy-start | bytes 1966084
  116.5 0.8 copy-start.4
  120.1 7.8 %collective-permute-start.4 = (bf16[5,64,256]{2,1,0:T(8,128)(2,1)}, bf16[5,64,256]{2,1,0:T(8,128)(2,1)S(1)}, u32[]{:S(2)}, u32[]{:S(2)}) collective-permute-start(bf16[5,64,256]{2,1,0:T(8,128)(2,1)} %get-tuple-element.18), channel_id=1, source_target_pairs={{0,8},{1,9},{2,10},{3,11},{4,12},{5,13},{6,14},{7,15},{8,0},{9,1},... | collective-permute-start | bytes 491528 | tf_op jit(solution)/shard_map/ppermute | solution.py:140
  120.7 14.8 %collective-permute-start.5 = (bf16[5,64,256]{2,1,0:T(8,128)(2,1)}, bf16[5,64,256]{2,1,0:T(8,128)(2,1)S(1)}, u32[]{:S(2)}, u32[]{:S(2)}) collective-permute-start(bf16[5,64,256]{2,1,0:T(8,128)(2,1)} %get-tuple-element.19), channel_id=1, source_target_pairs={{0,16},{1,17},{2,18},{3,19},{4,20},{5,21},{6,22},{7,23},{8,24},{9,... | collective-permute-start | bytes 491528 | tf_op jit(solution)/shard_map/ppermute | solution.py:140
  122.8 12.6 %collective-permute-start.6 = (bf16[5,64,256]{2,1,0:T(8,128)(2,1)}, bf16[5,64,256]{2,1,0:T(8,128)(2,1)S(1)}, u32[]{:S(2)}, u32[]{:S(2)}) collective-permute-start(bf16[5,64,256]{2,1,0:T(8,128)(2,1)} %get-tuple-element.20), channel_id=1, source_target_pairs={{0,24},{1,25},{2,26},{3,27},{4,28},{5,29},{6,30},{7,31},{8,16},{9,... | collective-permute-start | bytes 491528 | tf_op jit(solution)/shard_map/ppermute | solution.py:140
  127.9 7.5 %copy-start.5 = (bf16[5,64,256]{2,1,0:T(8,128)(2,1)}, bf16[5,64,256]{2,1,0:T(8,128)(2,1)S(1)}, u32[]{:S(2)}) copy-start(bf16[5,64,256]{2,1,0:T(8,128)(2,1)S(1)} %collective-permute-done.4.rest_1_) | copy-start | bytes 491524
  135.5 0.7 copy-start.6
  135.5 0.7 copy-start.7
Sparse Core Ops, SparseCore 0:
  10.2 63.8 all-gather.2
